TPU v7x, 128 devices: a whole 4x4x4 slice. The times are simulated.
128 devices in a mesh: group: 2 (over x_hi), gx: 8 (over x_lo, y), yz: 8 (over z, core).
Axes of the slice: x: 4 (x_hi: 2, x_lo: 2; x = x_hi * 2 + x_lo), y: 4, z: 4, core: 2. Of those that a mesh axis runs over, the one named last changes fastest.
Arguments:
- site_pos: float32 [2, 8, 8, 3, 16384], P('group', 'gx', 'yz'), may hold values from -6 to 6
- zone_id: int32 [2, 8, 8, 16384], P('group', 'gx', 'yz'), may hold values from 0 to 2, as said below
- site_eps: float32 [2, 8, 8, 16384], P('group', 'gx', 'yz'), may hold values from 0.5 to 1.5
- site_mass: float32 [2, 8, 8, 16384], P('group', 'gx', 'yz'), may hold values from 0.5 to 8
- neighbours: int32 [2, 8, 8, 16, 2048], P('group', 'gx', 'yz'), may hold values from 0 to 20480, as said below
- ghost_rows: int32 [2, 8, 8, 16384], P('group', 'gx', 'yz'), may hold values from 0 to 16383, as said below
- hyb_map: int32 [2, 8, 8, 8, 512], P('group', 'gx', 'yz'), may hold values from 0 to 16383, as said below
Outputs:
- forces: float32 [2, 8, 8, 3, 16384], P('group', 'gx', 'yz')
Inputs may be any that keep to these rules, and one draw needn't show every extreme that they name: `zone_id`: rows of group index 0 are 0 or 1, rows of group index 1 are 1 or 2. `neighbours`: each entry names a cluster tile of the device's lookup: 2048 local tiles, then nine blocks of 2048 ghost tiles by offsets along gx (outer) and yz (inner), then the padding tile at (163840) // 8. No entry names the block of offset (0, 0). `ghost_rows`: distinct rows of the device. `hyb_map`: on group index 0 all 4096 entries of a device are distinct; on group index 1 the 8 entries of a bead are equal and beads are distinct.
All inputs are finite; a program needn't handle non-finite values.
Results may differ from a plain program's by a relative error of at most 0.0003.
Values sent between devices are 32-bit elements; how exact they have to be, the bound alone decides.
A program may use at most 128 MiB of HBM per device.

v0:
```python
import jax
import jax.numpy as jnp
from jax import lax
from jax.sharding import PartitionSpec as P

CL = 8
NBS = 16


def extended(cells, sides, width):
    for axis, dim in sides:
        count = lax.axis_size(axis)
        head = lax.slice_in_dim(cells, 0, width, axis=dim)
        tail = lax.slice_in_dim(cells, cells.shape[dim] - width, cells.shape[dim], axis=dim)
        cells = jnp.concatenate(
            [
                lax.ppermute(tail, axis, [(i, (i + 1) % count) for i in range(count)]),
                cells,
                lax.ppermute(head, axis, [((i + 1) % count, i) for i in range(count)]),
            ],
            axis=dim,
        )
    return cells


def swapped(array, axis, distance):
    return lax.ppermute(array, axis, [(i, i ^ 1 << distance) for i in range(lax.axis_size(axis))])


def resolution(coord_x, zone_ids):
    middle = jax.nn.sigmoid(2.0 * coord_x)
    return jnp.where(zone_ids == 0, 1.0, jnp.where(zone_ids == 1, middle, 0.0))


def pair_curve(squared, group_id):
    return jnp.where(group_id == 0, 1.0 / (1.0 + squared) ** 3, jnp.exp(-0.5 * squared))


def short_range(positions, charges, lookup, cluster_lists, group_id):
    rows = positions.shape[1]
    tile_rows = lookup.shape[1] // CL
    clusters = rows // CL
    tile_table = jnp.transpose(lookup.reshape(4, tile_rows, CL), (1, 0, 2)).reshape(
        tile_rows, 4 * CL
    )
    pos_tiles = jnp.transpose(positions.reshape(3, clusters, CL), (0, 2, 1))
    charge_tiles = jnp.transpose(charges.reshape(clusters, CL), (1, 0))
    forces = jnp.zeros((3, CL, clusters), jnp.float32)
    stride = min(4, cluster_lists.shape[0])
    for begin_at in range(0, cluster_lists.shape[0], stride):
        picked = jnp.take(
            tile_table, cluster_lists[begin_at : begin_at + stride].reshape(-1), axis=0
        )
        chosen = jnp.transpose(picked.reshape(stride, clusters, 4, CL), (2, 3, 0, 1))
        offsets = pos_tiles[:, :, None, None, :] - chosen[:3, None]
        squared = jnp.sum(offsets * offsets, axis=0)
        weights = charge_tiles[:, None, None, :] * chosen[3][None] * pair_curve(squared, group_id)
        forces = forces + jnp.sum(weights[None] * offsets, axis=(2, 3))
    return jnp.transpose(forces, (0, 2, 1)).reshape(3, rows)


def site_payload(positions, resolved, scales, members):
    centres = jnp.sum(positions[:, members], axis=1) * 0.125
    site_lam = jnp.sum(resolved[members], axis=0) * 0.125
    site_scale = jnp.sum(scales[members], axis=0) * 0.125
    return jnp.concatenate([centres, site_lam[None], site_scale[None]], axis=0)


def coupling(mine_all, others):
    site_count = mine_all.shape[1]
    block_len = min(512, site_count)

    def coupling_one_block(begin_at):
        offsets = mine_all[:3, :, None] - others[:3, None, :]
        squared = jnp.sum(offsets * offsets, axis=0)
        weights = (
            mine_all[4][:, None]
            * others[4][None, :]
            * 0.5
            * (mine_all[3][:, None] + others[3][None, :])
            / (1.0 + squared) ** 2
        )
        return jnp.sum(weights[None] * offsets, axis=2) * (4.0 / site_count)

    starts = jnp.arange(site_count // block_len, dtype=jnp.int32) * block_len
    pieces = lax.map(coupling_one_block, starts)
    return jnp.moveaxis(pieces, 0, 1).reshape(3, site_count)


def spread(forces, site_pulls, members):
    shares = jnp.broadcast_to(site_pulls[:, None, :] * 0.125, (3,) + members.shape)
    return forces.at[:, members.reshape(-1)].add(shares.reshape(3, -1))


def bin_terms(coord_part, bin_count):
    centres = (jnp.arange(bin_count, dtype=jnp.float32) + 0.5) / NBS
    gap_rows = (coord_part[:, None] - centres[None, :]) * NBS
    return (jnp.exp(-0.5 * gap_rows * gap_rows), gap_rows)


def density(coords, masses, bin_count):
    rows_blk = min(4096, coords.shape[0])

    def density_one_block(begin_at):
        coord_part = lax.dynamic_slice_in_dim(coords, begin_at, rows_blk)
        mass_part = lax.dynamic_slice_in_dim(masses, begin_at, rows_blk)
        kernel, gap_rows = bin_terms(coord_part, bin_count)
        return jnp.sum(mass_part[:, None] * kernel, axis=0)

    starts = jnp.arange(coords.shape[0] // rows_blk, dtype=jnp.int32) * rows_blk
    return jnp.sum(lax.map(density_one_block, starts), axis=0)


def thermo_force(coords, resolved, deviation):
    rows_blk = min(4096, coords.shape[0])

    def thermo_one_block(begin_at):
        coord_part = lax.dynamic_slice_in_dim(coords, begin_at, rows_blk)
        kernel, gap_rows = bin_terms(coord_part, deviation.shape[0])
        return jnp.sum(kernel * gap_rows * deviation[None, :], axis=1)

    starts = jnp.arange(coords.shape[0] // rows_blk, dtype=jnp.int32) * rows_blk
    pushes = lax.map(thermo_one_block, starts).reshape(-1)
    return -4.0 * resolved * (1.0 - resolved) * pushes


def per_device(site_pos, zone_id, site_eps, site_mass, neighbours, ghost_rows, hyb_map):
    group_id = lax.axis_index("group")
    slab_at = lax.axis_index("gx")
    slab_count = lax.axis_size("gx")
    bin_count = NBS * lax.axis_size("group") * slab_count
    positions = site_pos[0, 0, 0]
    zone_ids = zone_id[0, 0, 0]
    scales = site_eps[0, 0, 0]
    masses = site_mass[0, 0, 0]
    row_lists = neighbours[0, 0, 0]
    ghosts = ghost_rows[0, 0, 0]
    members = hyb_map[0, 0, 0]
    resolved = resolution(positions[0], zone_ids)
    charges = scales * jnp.where(group_id == 0, resolved, 1.0 - resolved)
    coords = (group_id * slab_count + slab_at).astype(jnp.float32) + jax.nn.sigmoid(positions[0])
    profile = lax.psum(density(coords, masses, bin_count), ("group", "gx", "yz"))
    payload = jnp.concatenate([positions[:, ghosts], charges[ghosts][None]], axis=0)
    local_rows = jnp.concatenate([positions, charges[None]], axis=0)
    padding = jnp.zeros((4, CL), jnp.float32)
    received = extended(payload[:, None, None, :], (("gx", 1), ("yz", 2)), 1)
    received = received.reshape(received.shape[0], -1)
    lookup = jnp.concatenate([local_rows, received, padding], axis=1)
    forces = short_range(positions, charges, lookup, row_lists, group_id)
    own_sites = site_payload(positions, resolved, scales, members)
    partner = swapped(own_sites, "group", 0)
    site_pulls = coupling(own_sites, partner)
    forces = spread(forces, site_pulls, members)
    deviation = profile / (jnp.sum(profile) / bin_count) - 1.0
    pushes = thermo_force(coords, resolved, deviation)
    forces = forces.at[0].add(pushes)
    return forces[None, None, None]


def solution(mesh):
    return jax.shard_map(
        per_device,
        mesh=mesh,
        in_specs=(
            P("group", "gx", "yz", None, None),
            P("group", "gx", "yz", None),
            P("group", "gx", "yz", None),
            P("group", "gx", "yz", None),
            P("group", "gx", "yz", None, None),
            P("group", "gx", "yz", None),
            P("group", "gx", "yz", None, None),
        ),
        out_specs=P("group", "gx", "yz", None, None),
        check_vma=False,
    )
```

profile of v0, /device:TPU:1, one launch (start us, length us, event | category | flops | bytes accessed | tf_op | source)
XLA Modules:
  0.0 716.2 jit_solution(9039889594182424674)
XLA Ops:
  2.2 5.7 copy.172
  9.4 90.5 %gather_fusion.1 = f32[16384]{0:T(1024)S(1)} fusion(f32[16384]{0:T(1024)S(1)} %get-tuple-element.200, s32[16384]{0:T(1024)S(1)} %broadcast_clamp_fusion), kind=kCustom, calls=%fused_computation.5 | custom fusion | bytes 196608 | tf_op jit(solution)/shard_map/gather | solution.py:143
  100.0 57.8 %gather_fusion = f32[16384,3]{1,0:T(8,128)} fusion(f32[3,16384]{0,1:T(8,128)} %bitcast.122, s32[16384]{0:T(1024)S(1)} %broadcast_clamp_fusion), kind=kCustom, calls=%fused_computation.4 | custom fusion | bytes 458752 | tf_op jit(solution)/shard_map/gather | solution.py:143
  157.7 5.5 copy.174
  164.0 4.5 collective-permute-start.1
  168.6 23.0 %gather_fusion.2 = f32[4096]{0:T(1024)S(1)} fusion(f32[16384]{0:T(1024)S(1)} %bitcast.117, s32[4096]{0:T(1024)S(1)} %broadcast_clamp_fusion.1), kind=kCustom, calls=%fused_computation.6 | custom fusion | bytes 49152 | tf_op jit(solution)/shard_map/gather | solution.py:65
  191.6 14.1 %gather_fusion.3 = f32[4096,3]{1,0:T(8,128)S(1)} fusion(f32[3,16384]{0,1:T(8,128)} %bitcast.123, s32[4096]{0:T(1024)S(1)} %broadcast_clamp_fusion.1), kind=kCustom, calls=%fused_computation.7 | custom fusion | bytes 114688 | tf_op jit(solution)/shard_map/gather | solution.py:63
  205.8 23.0 %gather_fusion.4 = f32[4096]{0:T(1024)S(1)} fusion(f32[16384]{0:T(1024)S(1)} %get-tuple-element.201, s32[4096]{0:T(1024)S(1)} %broadcast_clamp_fusion.1), kind=kCustom, calls=%fused_computation.8 | custom fusion | bytes 49152 | tf_op jit(solution)/shard_map/gather | solution.py:64
  241.7 23.1 %while.29 = (s32[]{:T(128)}, f32[4,256]{1,0:T(4,128)S(1)}, s32[4]{0:T(128)S(1)}, f32[16384]{0:T(1024)}, f32[16384]{0:T(1024)S(1)}, /*index=5*/s32[]{:T(128)}, s32[]{:T(128)}, s32[]{:T(128)}) while((s32[]{:T(128)}, f32[4,256]{1,0:T(4,128)S(1)}, s32[4]{0:T(128)S(1)}, f32[16384]{0:T(1024)}, f32[16384]{0:T(1024)S(1)}, /*index=5*/s32[]{:T(128)}, ...), condition=%wide.region_16.18_spmd, body=%wide.region_14.17_spmd.sunk | while | flops 6291717 | bytes 103575 | solution.py:111
  264.8 67.5 %psum.7 = f32[256]{0:T(256)S(1)} all-reduce(f32[256]{0:T(256)S(1)} %reduce_sum.174), channel_id=1, replica_groups=mesh['group'=2,'gx'=8,'yz'=8] {'group','gx','yz'}, use_global_device_ids=true, to_apply=%region_18.20 | all-reduce | flops 256 | bytes 2048 | tf_op jit(solution)/shard_map/psum | solution.py:142
  333.6 24.0 %while.30 = (s32[]{:T(128)}, f32[4,4096]{1,0:T(4,128)}, s32[4]{0:T(128)S(1)}, f32[16384]{0:T(1024)S(1)}, f32[256]{0:T(256)S(1)}, /*index=5*/s32[]{:T(128)}, s32[]{:T(128)}, s32[]{:T(128)}) while((s32[]{:T(128)}, f32[4,4096]{1,0:T(4,128)}, s32[4]{0:T(128)S(1)}, f32[16384]{0:T(1024)S(1)}, f32[256]{0:T(256)S(1)}, /*index=5*/s32[]{:T(128)}, ...), condition=%wide.region_22.24_spmd, body=%wide.region_20.23_spmd.sunk | while | flops 7336453 | bytes 101523 | solution.py:123
  362.0 5.9 copy.173
  381.2 7.1 collective-permute-done.3
  390.0 4.6 maximum_maximum_fusion
  394.6 27.8 %reshape.457 = f32[4,20481,8]{2,1,0:T(8,128)} reshape(f32[4,163848]{1,0:T(4,128)S(1)} %maximum_maximum_fusion) | data formatting | bytes 5243136 | tf_op jit(solution)/shard_map/reshape | solution.py:43
  422.4 21.4 %copy.175 = f32[20481,4,8]{0,2,1:T(8,128)S(1)} copy(f32[20481,4,8]{2,0,1:T(8,128)} %bitcast.118) | data formatting | bytes 5243136 | tf_op jit(solution)/shard_map/transpose | solution.py:43
  443.8 6.1 copy.176
  449.9 31.8 %gather_fusion.8 = f32[8192,32]{1,0:T(8,128)} fusion(f32[20481,32]{1,0:T(8,128)} %copy.176, s32[8192]{0:T(1024)S(1)} %copy-done.12), kind=kCustom, calls=%fused_computation.3.clone | custom fusion | bytes 2129920 | tf_op jit(solution)/shard_map/jit(_take)/gather | solution.py:51
  481.8 7.4 %broadcast_select_fusion = f32[8192,32]{1,0:T(8,128)} fusion(f32[8192,32]{1,0:T(8,128)} %gather_fusion.8, pred[8192]{0:T(1024)(128)(4,1)S(1)} %copy-done.17), kind=kLoop, calls=%fused_computation.63 | loop fusion | flops 262144 | bytes 2105344 | tf_op jit(solution)/shard_map/jit(_take)/select_n | solution.py:51
  492.9 34.5 %gather_fusion.7 = f32[8192,32]{1,0:T(8,128)} fusion(f32[20481,32]{1,0:T(8,128)} %copy.176, s32[8192]{0:T(1024)} %fusion.40), kind=kCustom, calls=%fused_computation.2.clone | custom fusion | bytes 2129920 | tf_op jit(solution)/shard_map/jit(_take)/gather | solution.py:51
  527.4 7.4 %broadcast_select_fusion.1 = f32[8192,32]{1,0:T(8,128)} fusion(f32[8192,32]{1,0:T(8,128)} %gather_fusion.7, pred[8192]{0:T(1024)(128)(4,1)S(1)} %copy-done.18), kind=kLoop, calls=%fused_computation.64 | loop fusion | flops 262144 | bytes 2105344 | tf_op jit(solution)/shard_map/jit(_take)/select_n | solution.py:51
  540.1 34.5 %gather_fusion.5 = f32[8192,32]{1,0:T(8,128)} fusion(f32[20481,32]{1,0:T(8,128)} %copy.176, s32[8192]{0:T(1024)} %fusion.38), kind=kCustom, calls=%fused_computation.clone | custom fusion | bytes 2129920 | tf_op jit(solution)/shard_map/jit(_take)/gather | solution.py:51
  574.6 7.4 %broadcast_select_fusion.3 = f32[8192,32]{1,0:T(8,128)} fusion(f32[8192,32]{1,0:T(8,128)} %gather_fusion.5, pred[8192]{0:T(1024)(128)(4,1)S(1)} %copy-done.16), kind=kLoop, calls=%fused_computation.66 | loop fusion | flops 262144 | bytes 2105344 | tf_op jit(solution)/shard_map/jit(_take)/select_n | solution.py:51
  587.2 34.5 %gather_fusion.6 = f32[8192,32]{1,0:T(8,128)} fusion(f32[20481,32]{1,0:T(8,128)} %copy.176, s32[8192]{0:T(1024)} %fusion.39), kind=kCustom, calls=%fused_computation.1.clone | custom fusion | bytes 2129920 | tf_op jit(solution)/shard_map/jit(_take)/gather | solution.py:51
  621.8 7.4 %broadcast_select_fusion.2 = f32[8192,32]{1,0:T(8,128)} fusion(f32[8192,32]{1,0:T(8,128)} %gather_fusion.6, pred[8192]{0:T(1024)(128)(4,1)S(1)} %compare_and_fusion.2), kind=kLoop, calls=%fused_computation.65 | loop fusion | flops 262144 | bytes 2105344 | tf_op jit(solution)/shard_map/jit(_take)/select_n | solution.py:51
  638.9 4.3 fusion.12
  646.9 4.7 copy.193
  651.8 26.8 %scatter_fusion = f32[3,16384]{0,1:T(8,128)} fusion(f32[3,16384]{0,1:T(8,128)} %bitcast.119, s32[4096]{0:T(1024)S(1)} %bitcast.154, f32[4096,3]{1,0:T(8,128)S(1)} %bitcast.137), kind=kCustom, calls=%fused_computation.9 | custom fusion | flops 12288 | bytes 163840 | tf_op jit(solution)/shard_map/scatter-add | solution.py:92
  678.6 5.3 copy.200
  684.2 5.0 copy.198
  689.1 21.0 %scatter-add.13 = f32[1,1,1,3,16384]{3,4,2,1,0:T(8,128)} dynamic-update-slice(f32[1,1,1,3,16384]{3,4,2,1,0:T(8,128)} %bitcast.121, f32[1,1,1,1,16384]{3,4,2,1,0:T(8,128)} %copy.198, s32[]{:T(128)} %constant.188.clone.1, s32[]{:T(128)} %constant.188.clone.1, s32[]{:T(128)} %constant.188.clone.1, s32[]{:T(128)} %constant.188.clone.1, s32[]{:T(128)} %constant.188.clone.1) | dynamic-update-slice | bytes 131076 | tf_op jit(solution)/shard_map/scatter-add | solution.py:156
  710.2 5.9 copy.199
  (188 shorter events, 96.5 us)
Async XLA Ops:
  2.2 6.2 copy-start.3
  2.2 7.2 %copy-start = (f32[1,1,1,16384]{3,2,1,0:T(1,128)S(1)}, f32[1,1,1,16384]{3,2,1,0:T(1,128)}, u32[]{:S(2)}) copy-start(f32[1,1,1,16384]{3,2,1,0:T(1,128)} %param.17) | copy-start | bytes 196612
  157.7 10.8 %copy-start.15 = (s32[1,1,1,8,512]{4,3,2,1,0:T(8,128)S(1)}, s32[1,1,1,8,512]{4,3,2,1,0:T(8,128)}, u32[]{:S(2)}) copy-start(s32[1,1,1,8,512]{4,3,2,1,0:T(8,128)} %param.21) | copy-start | bytes 49156
  164.0 211.2 %collective-permute-start.1 = (f32[4,1,1,16384]{3,0,2,1:T(4,128)}, f32[4,1,1,16384]{3,0,2,1:T(4,128)}, u32[]{:S(2)}, u32[]{:S(2)}) collective-permute-start(f32[4,1,1,16384]{3,0,2,1:T(4,128)} %maximum_bitcast_fusion), channel_id=1, source_target_pairs={{8,0},{16,8},{24,16},{32,24},{40,32},{48,40},{56,48},{0,56},{9,1},... | collective-permute-start | bytes 786440 | tf_op jit(solution)/shard_map/ppermute | solution.py:19
  168.5 206.7 %collective-permute-start = (f32[4,1,1,16384]{3,0,2,1:T(4,128)}, f32[4,1,1,16384]{3,0,2,1:T(4,128)}, u32[]{:S(2)}, u32[]{:S(2)}) collective-permute-start(f32[4,1,1,16384]{3,0,2,1:T(4,128)} %maximum_bitcast_fusion), channel_id=1, source_target_pairs={{0,8},{8,16},{16,24},{24,32},{32,40},{40,48},{48,56},{56,0},{1,9},... | collective-permute-start | bytes 786440 | tf_op jit(solution)/shard_map/ppermute | solution.py:17
  205.8 27.3 %copy-start.11 = (s32[1,1,1,16,2048]{4,3,2,1,0:T(8,128)S(1)}, s32[1,1,1,16,2048]{4,3,2,1,0:T(8,128)}, u32[]{:S(2)}) copy-start(s32[1,1,1,16,2048]{4,3,2,1,0:T(8,128)} %param.19) | copy-start | bytes 393220
  228.8 7.4 %copy-start.8 = (s32[1,1,1,16384]{3,2,1,0:T(1,128)S(1)}, s32[1,1,1,16384]{3,2,1,0:T(1,128)}, u32[]{:S(2)}) copy-start(s32[1,1,1,16384]{3,2,1,0:T(1,128)} %param.16) | copy-start | bytes 196612
  229.2 3.9 copy-start.19
  229.2 3.9 copy-start.20
  229.8 143.8 %collective-permute-start.4 = (f32[5,512]{1,0:T(8,128)}, f32[5,512]{1,0:T(8,128)}, u32[]{:S(2)}, u32[]{:S(2)}) collective-permute-start(f32[5,512]{1,0:T(8,128)} %pad_maximum_fusion.2), channel_id=1, source_target_pairs={{0,64},{64,0},{1,65},{65,1},{2,66},{66,2},{3,67},{67,3},{4,68},{68... | collective-permute-start | bytes 30728 | tf_op jit(solution)/shard_map/ppermute | solution.py:27
  362.0 6.0 copy-start.14
  376.5 11.7 %collective-permute-start.3 = (f32[4,3,1,16384]{3,0,2,1:T(4,128)S(1)}, f32[4,3,1,16384]{3,0,2,1:T(4,128)S(1)}, u32[]{:S(2)}, u32[]{:S(2)}) collective-permute-start(f32[4,3,1,16384]{3,0,2,1:T(4,128)S(1)} %pad_maximum_fusion.1), channel_id=1, source_target_pairs={{1,0},{2,1},{3,2},{4,3},{5,4},{6,5},{7,6},{0,7},{9,8},{10,9},{11,1... | collective-permute-start | bytes 2359304 | tf_op jit(solution)/shard_map/ppermute | solution.py:19
  377.1 11.1 %collective-permute-start.2 = (f32[4,3,1,16384]{3,0,2,1:T(4,128)S(1)}, f32[4,3,1,16384]{3,0,2,1:T(4,128)S(1)}, u32[]{:S(2)}, u32[]{:S(2)}) collective-permute-start(f32[4,3,1,16384]{3,0,2,1:T(4,128)S(1)} %pad_maximum_fusion.1), channel_id=1, source_target_pairs={{0,1},{1,2},{2,3},{3,4},{4,5},{5,6},{6,7},{7,0},{8,9},{9,10},{10,1... | collective-permute-start | bytes 2359304 | tf_op jit(solution)/shard_map/ppermute | solution.py:17
  378.6 11.3 %copy-start.4 = (f32[3,16384]{1,0:T(4,128)S(1)}, f32[3,16384]{1,0:T(4,128)}, u32[]{:S(2)}) copy-start(f32[3,16384]{1,0:T(4,128)} %copy.173) | copy-start | bytes 589828
  378.6 11.3 %copy-start.9 = (f32[1,16384]{1,0:T(1,128)S(1)}, f32[1,16384]{1,0:T(1,128)}, u32[]{:S(2)}) copy-start(f32[1,16384]{1,0:T(1,128)} %fusion.36) | copy-start | bytes 196612
  443.8 6.1 copy-start.12
  449.9 31.9 %copy-start.17 = (pred[8192]{0:T(1024)(128)(4,1)S(1)}, pred[8192]{0:T(1024)(128)(4,1)}, u32[]{:S(2)}) copy-start(pred[8192]{0:T(1024)(128)(4,1)} %compare_and_fusion) | copy-start | bytes 24580
  492.9 34.5 %copy-start.18 = (pred[8192]{0:T(1024)(128)(4,1)S(1)}, pred[8192]{0:T(1024)(128)(4,1)}, u32[]{:S(2)}) copy-start(pred[8192]{0:T(1024)(128)(4,1)} %compare_and_fusion.1) | copy-start | bytes 24580
  540.1 34.5 %copy-start.16 = (pred[8192]{0:T(1024)(128)(4,1)S(1)}, pred[8192]{0:T(1024)(128)(4,1)}, u32[]{:S(2)}) copy-start(pred[8192]{0:T(1024)(128)(4,1)} %compare_and_fusion.3) | copy-start | bytes 24580
  633.1 1.1 copy-start.1
  633.1 1.6 copy-start.6
  633.1 1.8 copy-start.2
  633.2 2.2 copy-start.7
  646.9 4.8 copy-start.5
  646.9 4.9 copy-start.13
  678.6 5.3 copy-start.10
where the time goes:
time: 728 us; the launch traced here: 716 us
  local copies, waits for them, and re-layouts  508 us (70%)
  other arithmetic  108 us (15%)
  blocking collectives  67.5 us (9%)
  loops' own time  15.4 us (2%)
  starting transfers between devices  8.7 us (1%)
    gather x4, local copies, waits for them, and re-layouts, short_range(): jnp.take(tile_table, cluster_lists[begin_at:begin_at + stride].reshape(-1...  135 us
    gather x1, local copies, waits for them, and re-layouts, per_device(): charges[ghosts][None]  90.5 us
    psum x1, blocking collectives, per_device(): lax.psum(density(coords, masses, bin_count), ('group', 'gx', 'yz'))  67.5 us
    gather x2, local copies, waits for them, and re-layouts, per_device(): positions[:, ghosts]  63.2 us
    select_n x4, other arithmetic, short_range(): jnp.take(tile_table, cluster_lists[begin_at:begin_at + stride].reshape(-1...  29.8 us
    reshape x1, local copies, waits for them, and re-layouts, short_range(): lookup.reshape(4, tile_rows, CL)  27.8 us
    scatter-add x2, local copies, waits for them, and re-layouts, per_device(): forces = forces.at[0].add(pushes)  26.9 us
    scatter-add x1, other arithmetic, spread(): return forces.at[:, members.reshape(-1)].add(shares.reshape(3, -1))  26.8 us
  transfers between devices with their start and end apart: 5, of which 1 were waited for; matrix products, arithmetic and copies ran while one was open for 17% of the time, Pallas kernels for 0%

commit v1 on v0

v1 whole, which is shorter than its diff:
```python
import jax
import jax.numpy as jnp
from jax import lax
from jax.experimental import pallas as pl
from jax.experimental.pallas import tpu as pltpu
from jax.sharding import PartitionSpec as P

F32 = jnp.float32
MESH = pl.DeviceIdType.MESH
LANES = 128
PIECES = 4
NBS = 16
NEAR = NBS // 2


def iota(shape, dim):
    return lax.broadcasted_iota(jnp.int32, shape, dim)


def wide(row, rows=8):
    return jnp.broadcast_to(row, (rows, LANES))


def planes_of(pos_ref, planes):
    for k in range(3):
        for c in range(LANES):
            planes[k, c : c + 1, :] = pos_ref[k : k + 1, c * LANES : (c + 1) * LANES]


def dense_tiles(quad, out_ref, v):
    comp = (iota((8, LANES), 1) // 8) % 4
    for b in range(4):
        rolled = [quad[k] if k == b else pltpu.roll(quad[k], ((k - b) * 8) % LANES, 1) for k in range(4)]
        row = jnp.where(
            comp < 2,
            jnp.where(comp == 0, rolled[0], rolled[1]),
            jnp.where(comp == 2, rolled[2], rolled[3]),
        )
        out_ref[pl.ds(pl.multiple_of(v * 32 + b * 8, 8), 8), :] = row


def lane_pick(planes, count, ids, unroll, comps):
    hi = [i >> 7 for i in ids]
    lo = [i & 127 for i in ids]
    n = len(ids)

    def step(block, accs):
        accs = list(accs)
        for rr in range(unroll):
            r = block * unroll + rr
            same = [h == r for h in hi]
            for k in range(comps):
                src = wide(planes[k, pl.ds(r, 1), :])
                for i in range(n):
                    cand = jnp.take_along_axis(src, lo[i], axis=1)
                    accs[k * n + i] = jnp.where(same[i], cand, accs[k * n + i])
        return tuple(accs)

    zero = jnp.zeros((8, LANES), F32)
    if unroll == count:
        return step(0, (zero,) * (comps * n))
    return lax.fori_loop(0, count // unroll, step, (zero,) * (comps * n))


def prep_kernel(pos_ref, zone_ref, eps_ref, ghost_ref, pay_ref, local_ref, planes):
    group = lax.axis_index("group")
    planes_of(pos_ref, planes)

    def local(v, _):
        at = pl.ds(pl.multiple_of(v * 8, 8), 8)
        x = planes[0, at, :]
        zone = zone_ref[at, :]
        lam = jnp.where(zone == 0, 1.0, jnp.where(zone == 1, jax.nn.sigmoid(2.0 * x), 0.0))
        charge = eps_ref[at, :] * jnp.where(group == 0, lam, 1.0 - lam)
        planes[3, at, :] = charge
        dense_tiles([planes[k, at, :] for k in range(4)], local_ref, v)
        return 0

    lax.fori_loop(0, 16, local, 0)

    def ghosts(v, _):
        ids = [ghost_ref[pl.ds(pl.multiple_of(v * 16 + 8 * i, 8), 8), :] for i in range(2)]
        out = lane_pick(planes, LANES, ids, LANES, 4)
        for i in range(2):
            dense_tiles([out[k * 2 + i] for k in range(4)], pay_ref, v * 2 + i)
        return 0

    lax.fori_loop(0, 8, ghosts, 0)


def fold8(parts):
    sub = iota((8, LANES), 0)
    for bit in (1, 2, 4):
        low = (sub & bit) == 0
        parts = [
            jnp.where(low, one, two) + pltpu.roll(jnp.where(low, two, one), bit, 0)
            for one, two in zip(parts[::2], parts[1::2])
        ]
    return parts[0]


def edge_distance(t, slab, other):
    above = other > slab
    shift = jnp.where(above, (other - slab) * NBS, (slab - other - 1) * NBS).astype(F32)
    slope = jnp.where(above, -1.0, 1.0).astype(F32)
    return shift + slope * t


def weight_of(n):
    return jnp.exp(-0.5 * (n + 0.5) * (n + 0.5))


def order_of(slab, lane, row):
    k = row * LANES + lane
    slab_k = k // NBS
    n = k % NBS
    ahead = jnp.where(slab_k > slab, n, NBS - 1 - n)
    own = jnp.where(n < NEAR, NEAR + n, NBS - 1 - n)
    back = jnp.where(n < NEAR, NBS - 1 - n, n - NEAR)
    steps = jnp.where(slab_k == slab, n % NEAR, n)
    to = lane - n + jnp.where(slab_k == slab, own, ahead)
    return to, lane - n + jnp.where(slab_k == slab, back, ahead), steps


def density(planes, mass_ref, slab, sums, prof):
    def far(index, _):
        other = index + (index >= slab).astype(jnp.int32)
        accs = [jnp.zeros((8, LANES), F32)] * NBS
        for v in range(16):
            t = NBS * jax.nn.sigmoid(planes[0, v * 8 : v * 8 + 8, :])
            a = edge_distance(t, slab, other)
            q = jnp.exp(-a)
            term = mass_ref[v * 8 : v * 8 + 8, :] * jnp.exp(-0.5 * a * (a + 1.0))
            for n in range(NBS):
                accs[n] = accs[n] + term
                if n < NBS - 1:
                    term = term * q
        at = pl.multiple_of(other * NBS, NBS)
        sums[pl.ds(at, 8), :] = fold8(accs[:8])
        sums[pl.ds(at + 8, 8), :] = fold8(accs[8:])
        return 0

    lax.fori_loop(0, 15, far, 0)
    accs = [jnp.zeros((8, LANES), F32)] * NBS
    for v in range(16):
        u = NBS * jax.nn.sigmoid(planes[0, v * 8 : v * 8 + 8, :]) - NEAR
        mass = mass_ref[v * 8 : v * 8 + 8, :]
        for side, sign in ((0, 1.0), (1, -1.0)):
            q = jnp.exp(sign * u)
            term = mass * jnp.exp(-0.5 * u * (u - sign))
            for n in range(NEAR):
                accs[side * NEAR + n] = accs[side * NEAR + n] + term
                if n < NEAR - 1:
                    term = term * q
    at = pl.multiple_of(slab * NBS, NBS)
    sums[pl.ds(at, 8), :] = fold8(accs[:8])
    sums[pl.ds(at + 8, 8), :] = fold8(accs[8:])
    rows = []
    lane = iota((8, LANES), 1)
    for half in range(2):
        line = jnp.sum(sums[half * LANES : (half + 1) * LANES, :].T, axis=0, keepdims=True)
        _, source, steps = order_of(slab, lane, half)
        line = wide(line) * weight_of(steps.astype(F32))
        rows.append(jnp.take_along_axis(line, source, axis=1))
    sub = iota((8, LANES), 0)
    prof[...] = jnp.where(sub == 0, rows[0], jnp.where(sub == 1, rows[1], 0.0))


def coupling(mine, theirs, cols, pulls):
    for w in range(4):
        block = theirs[:, w * LANES : (w + 1) * LANES]
        cols[w * LANES : (w + 1) * LANES, :] = jnp.concatenate([block, jnp.zeros((LANES - 8, LANES), F32)], 0).T

    def step(r, accs):
        accs = list(accs)
        lot = cols[pl.ds(pl.multiple_of(r * 8, 8), 8), :]
        other = [jnp.broadcast_to(lot[:, k : k + 1], (8, LANES)) for k in range(5)]
        for w in range(4):
            own = [wide(mine[k : k + 1, w * LANES : (w + 1) * LANES]) for k in range(5)]
            d = [own[k] - other[k] for k in range(3)]
            near = 1.0 + (d[0] * d[0] + d[1] * d[1] + d[2] * d[2])
            weight = own[4] * other[4] * (own[3] + other[3]) / (near * near)
            for k in range(3):
                accs[w * 3 + k] = accs[w * 3 + k] + weight * d[k]
        return tuple(accs)

    accs = lax.fori_loop(0, 64, step, (jnp.zeros((8, LANES), F32),) * 12)
    for w in range(4):
        for k in range(3):
            pulls[k : k + 1, w * LANES : (w + 1) * LANES] = jnp.sum(accs[w * 3 + k], axis=0, keepdims=True) * (0.5 * 4.0 / 512)


def spread(pulls, hyb_ref, out):
    total = jnp.zeros((6 * LANES, LANES), F32)
    sub = iota((LANES, 512), 0)
    shares = []
    for k in range(3):
        share = pulls[k : k + 1, :] * 0.125
        high = share.astype(jnp.bfloat16).astype(F32)
        shares += [high, share - high]
    for m in range(8):
        rows = hyb_ref[m : m + 1, :]
        hit = jnp.broadcast_to(rows >> 7, (LANES, 512)) == sub
        lot = jnp.broadcast_to(rows & 127, (LANES, 512)) == sub
        left = jnp.concatenate([jnp.where(hit, jnp.broadcast_to(s, (LANES, 512)), 0.0).astype(jnp.bfloat16) for s in shares], 0)
        right = jnp.where(lot, 1.0, 0.0).astype(jnp.bfloat16)
        total = total + lax.dot_general(left, right, (((1,), (1,)), ((), ())), preferred_element_type=F32)
    for k in range(3):
        out[k] = total[2 * k * LANES : (2 * k + 1) * LANES] + total[(2 * k + 1) * LANES : (2 * k + 2) * LANES]


def comm_kernel(
    pay_ref, pos_ref, zone_ref, eps_ref, mass_ref, hyb_ref,
    blocks_ref, prof_ref, spread_ref,
    planes, sums, part1, part2, got1, got2, mine, theirs, cols, pulls,
    send_sem, recv_sem, s1, r1, s2, r2, ss, sr,
):
    group, slab_at, column = lax.axis_index("group"), lax.axis_index("gx"), lax.axis_index("yz")
    slab = group * 8 + slab_at

    def in_column(d):
        return (group, slab_at, lax.rem(column + d, 8))

    def across(d):
        return (lax.rem(group + d // 8, 2), lax.rem(slab_at + d % 8, 8), column)

    barrier = pltpu.get_barrier_semaphore()
    for d in range(1, 8):
        pl.semaphore_signal(barrier, inc=1, device_id=in_column(d), device_id_type=MESH)
    for d in range(1, 16):
        pl.semaphore_signal(barrier, inc=1, device_id=across(d), device_id_type=MESH)
    pl.semaphore_wait(barrier, 22)

    step = 512 // PIECES
    routes = (
        (1, None, across(1)),
        (7, None, across(7)),
        (3, None, in_column(1)),
        (5, None, in_column(7)),
        (0, 1, in_column(1)),
        (2, 1, in_column(7)),
        (6, 7, in_column(1)),
        (8, 7, in_column(7)),
    )

    def copy(index, p):
        block, source, target = routes[index]
        rows = pl.ds(p * step, step)
        src = pay_ref.at[rows] if source is None else blocks_ref.at[source, rows]
        return pltpu.make_async_remote_copy(
            src_ref=src, dst_ref=blocks_ref.at[block, rows],
            send_sem=send_sem.at[index, p], recv_sem=recv_sem.at[index, p],
            device_id=target, device_id_type=MESH,
        )

    own_copies = [(i, p) for p in range(PIECES) for i in (0, 1, 2, 3)]
    for i, p in own_copies:
        copy(i, p).start()

    planes_of(pos_ref, planes)
    density(planes, mass_ref, slab, sums, part1)

    def share1(d):
        return pltpu.make_async_remote_copy(
            src_ref=part1, dst_ref=got1.at[d], send_sem=s1.at[d], recv_sem=r1.at[d],
            device_id=in_column(d), device_id_type=MESH)

    def share2(d):
        return pltpu.make_async_remote_copy(
            src_ref=part2, dst_ref=got2.at[d], send_sem=s2.at[d], recv_sem=r2.at[d],
            device_id=across(d), device_id_type=MESH)

    for d in range(1, 8):
        share1(d).start()

    def forward(p):
        for first, lot in ((0, (4, 5)), (1, (6, 7))):
            copy(first, p).wait_recv()
            for i in lot:
                copy(i, p).start()

    forward(0)

    def resolve(v, _):
        at = pl.ds(pl.multiple_of(v * 8, 8), 8)
        zone = zone_ref[at, :]
        planes[3, at, :] = jnp.where(zone == 0, 1.0, jnp.where(zone == 1, jax.nn.sigmoid(2.0 * planes[0, at, :]), 0.0))
        planes[4, at, :] = eps_ref[at, :]
        return 0

    lax.fori_loop(0, 16, resolve, 0)
    mine[...] = jnp.zeros_like(mine)
    for w in range(4):
        ids = [hyb_ref[:, w * LANES : (w + 1) * LANES]]
        out = lane_pick(planes, LANES, ids, 32, 5)
        for k in range(5):
            mine[k : k + 1, w * LANES : (w + 1) * LANES] = jnp.sum(out[k], axis=0, keepdims=True) * 0.125
    swap = pltpu.make_async_remote_copy(
        src_ref=mine, dst_ref=theirs, send_sem=ss, recv_sem=sr, device_id=across(8), device_id_type=MESH)
    swap.start()
    forward(1)
    for d in range(1, 8):
        share1(d).wait_recv()
    total = part1[...]
    for d in range(1, 8):
        total = total + got1[d]
    part2[...] = total
    for d in range(1, 16):
        share2(d).start()
    forward(2)
    swap.wait_recv()
    coupling(mine, theirs, cols, pulls)
    forward(3)
    spread(pulls, hyb_ref, spread_ref)
    for d in range(1, 16):
        share2(d).wait_recv()
    total = part2[...]
    for d in range(1, 16):
        total = total + got2[d]
    prof_ref[...] = total
    for p in range(PIECES):
        for i in range(2, 8):
            copy(i, p).wait_recv()
    for p in range(PIECES):
        for i in range(8):
            copy(i, p).wait_send()
    for d in range(1, 8):
        share1(d).wait_send()
    for d in range(1, 16):
        share2(d).wait_send()
    swap.wait_send()


def force_kernel(
    nb_ref, local_ref, blocks_ref, prof_ref, spread_ref, pos_ref, zone_ref, eps_ref,
    out_ref,
    table, planes, turned, gathered, lot_ref, forces, push, coef_a, coef_b,
):
    group = lax.axis_index("group")
    slab = group * 8 + lax.axis_index("gx")
    planes_of(pos_ref, planes)
    lane = iota((8, LANES), 1)
    quarter = lane // 32

    def fill(source, block):
        def one(r, _):
            rows = source[pl.ds(pl.multiple_of(r * 8, 8), 8), :]
            rolled = [rows] + [pltpu.roll(rows, 32 * k, 1) for k in (1, 2, 3)]
            at = block * 2048 + (r // 4) * 128 + r % 4
            for q in range(4):
                tile = jnp.where(
                    quarter < 2,
                    jnp.where(quarter == 0, rolled[-q % 4], rolled[(1 - q) % 4]),
                    jnp.where(quarter == 2, rolled[(2 - q) % 4], rolled[(3 - q) % 4]),
                )
                table[pl.ds(at + q * 4, 8, stride=16), :] = tile
            return 0

        lax.fori_loop(0, 64, one, 0, unroll=4)

    fill(local_ref, 0)
    for block in range(9):
        if block != 4:
            fill(blocks_ref.at[block], block + 1)
    table[20480:20488, :] = jnp.zeros((8, LANES), F32)

    def resolve(v, _):
        at = pl.ds(pl.multiple_of(v * 8, 8), 8)
        zone = zone_ref[at, :]
        lam = jnp.where(zone == 0, 1.0, jnp.where(zone == 1, jax.nn.sigmoid(2.0 * planes[0, at, :]), 0.0))
        planes[3, at, :] = eps_ref[at, :] * jnp.where(group == 0, lam, 1.0 - lam)
        planes[4, at, :] = -4.0 * lam * (1.0 - lam)
        return 0

    lax.fori_loop(0, 16, resolve, 0)
    for k in range(4):
        turned[k] = planes[k].T

    profile = prof_ref[...]
    mean = jnp.sum(profile) / 256.0
    for half in range(2):
        source, _, steps = order_of(slab, lane, half)
        steps = steps.astype(F32)
        dev = wide(profile[half : half + 1, :] / mean - 1.0)
        dev = jnp.take_along_axis(dev, source, axis=1) * weight_of(steps)
        coef_a[half * LANES : (half + 1) * LANES, :] = wide(dev[0:1, :], LANES).T
        coef_b[half * LANES : (half + 1) * LANES, :] = wide((dev * steps)[0:1, :], LANES).T

    def horner(q, start, count):
        a = wide(coef_a[pl.ds(start + count - 1, 1), :])
        b = wide(coef_b[pl.ds(start + count - 1, 1), :])
        for n in range(count - 2, -1, -1):
            a = a * q + wide(coef_a[pl.ds(start + n, 1), :])
            b = b * q + wide(coef_b[pl.ds(start + n, 1), :])
        return a, b

    def thermo(v):
        at = pl.ds(pl.multiple_of(v * 8, 8), 8)
        t = NBS * jax.nn.sigmoid(planes[0, at, :])
        total = jnp.zeros((8, LANES), F32)
        for index in range(15):
            other = index + (index >= slab).astype(jnp.int32)
            dist = edge_distance(t, slab, other)
            a, b = horner(jnp.exp(-dist), other * NBS, NBS)
            part = jnp.exp(-0.5 * dist * (dist + 1.0)) * ((dist + 0.5) * a + b)
            total = total + jnp.where(other > slab, -part, part)
        u = t - NEAR
        a, b = horner(jnp.exp(u), slab * NBS, NEAR)
        total = total + jnp.exp(-0.5 * u * (u - 1.0)) * ((u - 0.5) * a - b)
        a, b = horner(jnp.exp(-u), slab * NBS + NEAR, NEAR)
        total = total + jnp.exp(-0.5 * u * (u + 1.0)) * ((u + 0.5) * a + b)
        push[at, :] = planes[4, at, :] * total

    def run(curve):
        def body(cl, _):
            own = [[wide(turned[k, pl.ds(cl * 8 + i, 1), :]) for i in range(8)] for k in range(3)]
            accs = [[jnp.zeros((8, LANES), F32)] * 8 for _ in range(3)]
            for quad in range(4):
                buf = quad % 2
                for g in range(4):
                    slot = quad * 4 + g
                    for c in range(LANES):
                        tile = nb_ref.at[pl.ds(slot * 2048 + c * 16, 16)][cl]
                        gathered[buf, c : c + 1, 32 * g : 32 * g + 32] = table[pl.ds(tile, 1), 32 * g : 32 * g + 32]
                lot = gathered[buf].T
                for g in range(4):
                    x, y, z, c = [lot[32 * g + 8 * k : 32 * g + 8 * k + 8] for k in range(4)]
                    for i in range(8):
                        dx, dy, dz = own[0][i] - x, own[1][i] - y, own[2][i] - z
                        w = c * curve(dx * dx + dy * dy + dz * dz)
                        accs[0][i] = accs[0][i] + w * dx
                        accs[1][i] = accs[1][i] + w * dy
                        accs[2][i] = accs[2][i] + w * dz
            at = pl.ds(pl.multiple_of(cl * 8, 8), 8)
            charge = turned[3, at, :]
            for k in range(3):
                forces[k, at, :] = charge * fold8(accs[k])
            thermo(cl)
            return 0

        lax.fori_loop(0, 16, body, 0)

    def soft(s):
        r = 1.0 / (1.0 + s)
        return r * r * r

    @pl.when(group == 0)
    def _():
        run(soft)

    @pl.when(group != 0)
    def _():
        run(lambda s: jnp.exp(-0.5 * s))

    for k in range(3):
        plane = forces[k].T + spread_ref[k]
        if k == 0:
            plane = plane + push[...]
        planes[k] = plane
    for k in range(3):
        for c in range(LANES):
            out_ref[k : k + 1, c * LANES : (c + 1) * LANES] = planes[k, c : c + 1, :]


VMEM = pl.BlockSpec(memory_space=pltpu.VMEM)
ANY = pl.BlockSpec(memory_space=pl.ANY)
SMEM = pl.BlockSpec(memory_space=pltpu.SMEM)


def shape(*dims):
    return jax.ShapeDtypeStruct(dims, F32)


def per_device(site_pos, zone_id, site_eps, site_mass, neighbours, ghost_rows, hyb_map):
    pos = site_pos.reshape(3, 16384)
    zone = zone_id.reshape(128, 128)
    eps = site_eps.reshape(128, 128)
    mass = site_mass.reshape(128, 128)
    lists = neighbours.reshape(32768)
    ghost = ghost_rows.reshape(128, 128)
    hyb = hyb_map.reshape(8, 512)
    pay, local = pl.pallas_call(
        prep_kernel,
        out_shape=(shape(512, 128), shape(512, 128)),
        in_specs=[VMEM] * 4,
        out_specs=(VMEM, VMEM),
        scratch_shapes=[pltpu.VMEM((4, 128, 128), F32)],
        compiler_params=pltpu.CompilerParams(vmem_limit_bytes=40 * 2**20),
        name="prep",
    )(pos, zone, eps, ghost)
    blocks, prof, extra = pl.pallas_call(
        comm_kernel,
        out_shape=(shape(9, 512, 128), shape(8, 128), shape(3, 128, 128)),
        in_specs=[ANY] + [VMEM] * 5,
        out_specs=(ANY, VMEM, VMEM),
        scratch_shapes=[
            pltpu.VMEM((5, 128, 128), F32),
            pltpu.VMEM((256, 128), F32),
            pltpu.VMEM((8, 128), F32),
            pltpu.VMEM((8, 128), F32),
            pltpu.VMEM((8, 8, 128), F32),
            pltpu.VMEM((16, 8, 128), F32),
            pltpu.VMEM((8, 512), F32),
            pltpu.VMEM((8, 512), F32),
            pltpu.VMEM((512, 128), F32),
            pltpu.VMEM((8, 512), F32),
            pltpu.SemaphoreType.DMA((8, PIECES)),
            pltpu.SemaphoreType.DMA((8, PIECES)),
            pltpu.SemaphoreType.DMA((8,)),
            pltpu.SemaphoreType.DMA((8,)),
            pltpu.SemaphoreType.DMA((16,)),
            pltpu.SemaphoreType.DMA((16,)),
            pltpu.SemaphoreType.DMA,
            pltpu.SemaphoreType.DMA,
        ],
        compiler_params=pltpu.CompilerParams(
            collective_id=0, has_side_effects=True, vmem_limit_bytes=40 * 2**20
        ),
        name="exchange",
    )(pay, pos, zone, eps, mass, hyb)
    forces = pl.pallas_call(
        force_kernel,
        out_shape=shape(3, 16384),
        in_specs=[SMEM] + [VMEM] * 7,
        out_specs=VMEM,
        scratch_shapes=[
            pltpu.VMEM((20488, 128), F32),
            pltpu.VMEM((5, 128, 128), F32),
            pltpu.VMEM((4, 128, 128), F32),
            pltpu.VMEM((2, 128, 128), F32),
            pltpu.VMEM((8, 128), F32),
            pltpu.VMEM((3, 128, 128), F32),
            pltpu.VMEM((128, 128), F32),
            pltpu.VMEM((256, 128), F32),
            pltpu.VMEM((256, 128), F32),
        ],
        compiler_params=pltpu.CompilerParams(vmem_limit_bytes=48 * 2**20),
        name="forces",
    )(lists, local, blocks, prof, extra, pos, zone, eps)
    return forces.reshape(1, 1, 1, 3, 16384)


def solution(mesh):
    return jax.shard_map(
        per_device,
        mesh=mesh,
        in_specs=(
            P("group", "gx", "yz", None, None),
            P("group", "gx", "yz", None),
            P("group", "gx", "yz", None),
            P("group", "gx", "yz", None),
            P("group", "gx", "yz", None, None),
            P("group", "gx", "yz", None),
            P("group", "gx", "yz", None, None),
        ),
        out_specs=P("group", "gx", "yz", None, None),
        check_vma=False,
    )
```

time: 728 us -> 96.3 us (0.13); the launches traced: 716 us -> 95.8 us
  local copies, waits for them, and re-layouts: 508 us -> 8.61 us
  other arithmetic: 108 us -> 0 us
  Pallas kernels: 0 us -> 87.1 us
  blocking collectives: 67.5 us -> 0 us
  loops' own time: 15.4 us -> 0 us
  starting transfers between devices: 8.7 us -> 0 us
    gather x12 -> x0, local copies, waits for them, and re-layouts: 349 us -> none  [the longest x4 135 us: short_range(): jnp.take(tile_table, cluster_lists[begin_at:begin_at + stride].reshape(-1...]
    pallas_call x0 -> x3, Pallas kernels: none -> 87.1 us  [the longest x1 44.1 us: per_device(): pl.pallas_call(force_kernel, out_shape=shape(3, 16384), in_specs=[SMEM] +...]
    psum x1 -> x0, blocking collectives: 67.5 us -> none  [per_device(): lax.psum(density(coords, masses, bin_count), ('group', 'gx', 'yz'))]
    reshape x6 -> x1, local copies, waits for them, and re-layouts: 36.8 us -> 0.88 us  [per_device(): return forces.reshape(1, 1, 1, 3, 16384)]
    select_n x6 -> x0, other arithmetic: 31.3 us -> none  [the longest x4 29.8 us: short_range(): jnp.take(tile_table, cluster_lists[begin_at:begin_at + stride].reshape(-1...]
    scatter-add x2 -> x0, local copies, waits for them, and re-layouts: 26.9 us -> none  [per_device(): forces = forces.at[0].add(pushes)]
    scatter-add x1 -> x0, other arithmetic: 26.8 us -> none  [spread(): return forces.at[:, members.reshape(-1)].add(shares.reshape(3, -1))]
    reduce_sum x18 -> x0, other arithmetic: 26.3 us -> none  [the longest x4 9.25 us: density_one_block(): return jnp.sum(mass_part[:, None] * kernel, axis=0)]
  transfers between devices with their start and end apart: 5 -> 0, of which waited for: 1 -> 0; matrix products, arithmetic and copies ran while one was open for 17% -> 0% of each run, Pallas kernels for 0% -> 0%
where the time goes in v1:
time: 96.3 us; the launch traced here: 95.8 us
  Pallas kernels  87.1 us (90%)
  local copies, waits for them, and re-layouts  8.61 us (9%)
    pallas_call x1, Pallas kernels, per_device(): pl.pallas_call(force_kernel, out_shape=shape(3, 16384), in_specs=[SMEM] +...  44.1 us
    pallas_call x1, Pallas kernels, per_device(): pl.pallas_call(comm_kernel, out_shape=(shape(9, 512, 128), shape(8, 128),...  31.2 us
    pallas_call x1, Pallas kernels, per_device(): pl.pallas_call(prep_kernel, out_shape=(shape(512, 128), shape(512, 128)),...  11.8 us
    unnamed x16, local copies, waits for them, and re-layouts  7.73 us

profile of v1, /device:TPU:1, one launch (start us, length us, event | category | flops | bytes accessed | tf_op | source)
XLA Modules:
  0.0 95.8 jit_solution(4035595663040096835)
XLA Ops:
  0.0 1.1 %copy.12 = f32[1,1,1,3,16384]{4,3,2,1,0:T(4,128)S(1)} copy(f32[1,1,1,3,16384]{4,2,3,1,0:T(1,128)} %param.7) | data formatting | bytes 393216
  1.1 0.0 copy-start
  1.1 0.8 copy-done
  1.9 0.0 copy-start.2
  1.9 0.8 copy-done.2
  2.7 0.0 copy-start.4
  2.8 0.8 copy-done.4
  3.6 11.8 %prep.1 = (f32[512,128]{1,0:T(8,128)S(1)}, f32[512,128]{1,0:T(8,128)S(1)}) custom-call(f32[3,16384]{1,0:T(4,128)S(1)} %bitcast.11, s32[128,128]{1,0:T(8,128)S(1)} %bitcast.15, f32[128,128]{1,0:T(8,128)S(1)} %bitcast.18, s32[128,128]{1,0:T(8,128)S(1)} %bitcast.22), custom_call_target="tpu_custom_call" | custom-call | tf_op jit(solution)/shard_map/prep/pallas_call | solution.py:482
  15.4 0.0 copy-start.5
  15.4 0.8 copy-done.5
  16.2 0.0 copy-start.6
  16.2 0.7 copy-done.6
  16.9 31.2 %exchange.1 = (f32[9,512,128]{2,1,0:T(8,128)S(1)}, f32[8,128]{1,0:T(8,128)S(1)}, f32[3,128,128]{2,1,0:T(8,128)S(1)}) custom-call(f32[512,128]{1,0:T(8,128)S(1)} %get-tuple-element.11.pay_ref, f32[3,16384]{1,0:T(4,128)S(1)} %bitcast.12, s32[128,128]{1,0:T(8,128)S(1)} %bitcast.16, f32[128,128]{1,0:T(8,128)S(1)} %bitcast.19, f32[128,128]{1,0:T(8,128)S(1)} %bitcast.23, ...), custom_call_target="tpu_custom_call" | custom-call | tf_op jit(solution)/shard_map/exchange/pallas_call | solution.py:491
  48.1 0.9 copy.10
  49.1 0.0 copy-start.1
  49.1 0.8 copy-done.1
  49.9 0.0 copy-start.3
  49.9 0.8 copy-done.3
  50.7 44.1 %forces.1 = f32[3,16384]{1,0:T(4,128)S(1)} custom-call(s32[32768]{0:T(1024)S(1)} %bitcast.21, f32[512,128]{1,0:T(8,128)S(1)} %get-tuple-element.10.local_ref, f32[9,512,128]{2,1,0:T(8,128)S(1)} %get-tuple-element.12.blocks_ref, f32[8,128]{1,0:T(8,128)S(1)} %get-tuple-element.13.prof_ref, f32[3,128,128]{2,1,0:T(8,128)S(1)} %get-tuple-element.14.spread_ref, ...), custom_call_target="tpu_custom_call" | custom-call | tf_op jit(solution)/shard_map/forces/pallas_call | solution.py:521
  94.9 0.9 copy.8
Async XLA Ops:
  1.1 0.8 copy-start
  1.9 0.8 copy-start.2
  2.7 0.8 copy-start.4
  15.4 0.8 copy-start.5
  16.2 0.7 copy-start.6
  49.1 0.8 copy-start.1
  49.9 0.8 copy-start.3

commit v2 on v1

v2 whole, which is shorter than its diff:
```python
import jax
import jax.numpy as jnp
from jax import lax
from jax.experimental import pallas as pl
from jax.experimental.pallas import tpu as pltpu
from jax.sharding import PartitionSpec as P

F32 = jnp.float32
MESH = pl.DeviceIdType.MESH
LANES = 128
PIECES = 4
NBS = 16
NEAR = NBS // 2


def iota(shape, dim):
    return lax.broadcasted_iota(jnp.int32, shape, dim)


def wide(row, rows=8):
    return jnp.broadcast_to(row, (rows, LANES))


def dense_tiles(quad, out_ref, v):
    comp = (iota((8, LANES), 1) // 8) % 4
    for b in range(4):
        rolled = [quad[k] if k == b else pltpu.roll(quad[k], ((k - b) * 8) % LANES, 1) for k in range(4)]
        row = jnp.where(
            comp < 2,
            jnp.where(comp == 0, rolled[0], rolled[1]),
            jnp.where(comp == 2, rolled[2], rolled[3]),
        )
        out_ref[pl.ds(pl.multiple_of(v * 32 + b * 8, 8), 8), :] = row


def lane_pick(planes, ids, beside):
    hi = [i >> 7 for i in ids]
    lo = [i & 127 for i in ids]
    out = [[jnp.zeros((8, LANES), F32)] * 4 for _ in ids]
    for r in range(LANES):
        same = [h == r for h in hi]
        for k in range(4):
            src = wide(planes[k, r : r + 1, :])
            for i in range(len(ids)):
                out[i][k] = jnp.where(same[i], jnp.take_along_axis(src, lo[i], axis=1), out[i][k])
        beside(r)
    return out


def fold8(parts):
    sub = iota((8, LANES), 0)
    for bit in (1, 2, 4):
        low = (sub & bit) == 0
        parts = [
            jnp.where(low, one, two) + pltpu.roll(jnp.where(low, two, one), bit, 0)
            for one, two in zip(parts[::2], parts[1::2])
        ]
    return parts[0]


def edge_distance(t, slab, other):
    above = other > slab
    shift = jnp.where(above, (other - slab) * NBS, (slab - other - 1) * NBS).astype(F32)
    slope = jnp.where(above, -1.0, 1.0).astype(F32)
    return shift + slope * t


def weight_of(n):
    return jnp.exp(-0.5 * (n + 0.5) * (n + 0.5))


def order_of(slab, lane, row):
    k = row * LANES + lane
    slab_k = k // NBS
    n = k % NBS
    ahead = jnp.where(slab_k > slab, n, NBS - 1 - n)
    own = jnp.where(n < NEAR, NEAR + n, NBS - 1 - n)
    back = jnp.where(n < NEAR, NBS - 1 - n, n - NEAR)
    steps = jnp.where(slab_k == slab, n % NEAR, n)
    to = lane - n + jnp.where(slab_k == slab, own, ahead)
    return to, lane - n + jnp.where(slab_k == slab, back, ahead), steps


def far_term(bins, mass, accs, slab, other, v):
    a = edge_distance(bins[v * 8 : v * 8 + 8, :], slab, other)
    q = jnp.exp(-a)
    term = mass[v * 8 : v * 8 + 8, :] * jnp.exp(-0.5 * a * (a + 1.0))
    for n in range(NBS):
        accs[n] = accs[n] + term
        if n < NBS - 1:
            term = term * q


def keep_bins(sums, slab, accs):
    at = pl.multiple_of(slab * NBS, NBS)
    sums[pl.ds(at, 8), :] = fold8(accs[:8])
    sums[pl.ds(at + 8, 8), :] = fold8(accs[8:])


def density(bins, mass, slab, sums, prof):
    accs = [jnp.zeros((8, LANES), F32)] * NBS
    for v in range(16):
        u = bins[v * 8 : v * 8 + 8, :] - NEAR
        for side, sign in ((0, 1.0), (1, -1.0)):
            q = jnp.exp(sign * u)
            term = mass[v * 8 : v * 8 + 8, :] * jnp.exp(-0.5 * u * (u - sign))
            for n in range(NEAR):
                accs[side * NEAR + n] = accs[side * NEAR + n] + term
                if n < NEAR - 1:
                    term = term * q
    keep_bins(sums, slab, accs)
    rows = []
    lane = iota((8, LANES), 1)
    for half in range(2):
        line = jnp.sum(sums[half * LANES : (half + 1) * LANES, :].T, axis=0, keepdims=True)
        _, source, steps = order_of(slab, lane, half)
        line = wide(line) * weight_of(steps.astype(F32))
        rows.append(jnp.take_along_axis(line, source, axis=1))
    sub = iota((8, LANES), 0)
    prof[...] = jnp.where(sub == 0, rows[0], jnp.where(sub == 1, rows[1], 0.0))


def site_tables(planes, tables):
    for i, k in enumerate((0, 1, 2, 4, 5)):
        turned = planes[k].T
        rest = jnp.concatenate([turned[:64], turned[64:]], axis=1)
        for part in range(3):
            term = rest.astype(jnp.bfloat16)
            tables[part, i * 64 : i * 64 + 64, :] = term
            rest = rest - term.astype(F32)


def member_sites(hyb_ref, tables, sites, m):
    rows = hyb_ref[pl.ds(m, 1), :]
    upper = ((rows >> 6) & 1) * LANES + (rows >> 7)
    hot = jnp.where(jnp.broadcast_to(upper, (256, 512)) == iota((256, 512), 0), 1.0, 0.0).astype(jnp.bfloat16)
    found = jnp.dot(tables[0], hot, preferred_element_type=F32)
    found = found + jnp.dot(tables[1], hot, preferred_element_type=F32)
    found = found + jnp.dot(tables[2], hot, preferred_element_type=F32)
    pick = jnp.broadcast_to(rows & 63, (64, 512)) == iota((64, 512), 0)
    for k in range(5):
        chosen = jnp.where(pick, found[k * 64 : k * 64 + 64], 0.0)
        total = sites[k]
        for j in range(8):
            total = total + chosen[j * 8 : j * 8 + 8]
        sites[k] = total


def coupling(mine, theirs, cols, pulls):
    for w in range(4):
        block = theirs[:, w * LANES : (w + 1) * LANES]
        cols[w * LANES : (w + 1) * LANES, :] = jnp.concatenate([block, jnp.zeros((LANES - 8, LANES), F32)], 0).T

    def step(r, accs):
        accs = list(accs)
        lot = cols[pl.ds(pl.multiple_of(r * 8, 8), 8), :]
        other = [jnp.broadcast_to(lot[:, k : k + 1], (8, LANES)) for k in range(5)]
        for w in range(4):
            own = [wide(mine[k : k + 1, w * LANES : (w + 1) * LANES]) for k in range(5)]
            d = [own[k] - other[k] for k in range(3)]
            near = 1.0 + (d[0] * d[0] + d[1] * d[1] + d[2] * d[2])
            weight = own[4] * other[4] * (own[3] + other[3]) / (near * near)
            for k in range(3):
                accs[w * 3 + k] = accs[w * 3 + k] + weight * d[k]
        return tuple(accs)

    accs = lax.fori_loop(0, 64, step, (jnp.zeros((8, LANES), F32),) * 12)
    for w in range(4):
        for k in range(3):
            pulls[k : k + 1, w * LANES : (w + 1) * LANES] = jnp.sum(accs[w * 3 + k], axis=0, keepdims=True) * (0.5 * 4.0 / 512)


def spread(pulls, hyb_ref, out):
    total = jnp.zeros((6 * LANES, LANES), F32)
    sub = iota((LANES, 512), 0)
    shares = []
    for k in range(3):
        share = pulls[k : k + 1, :] * 0.125
        high = share.astype(jnp.bfloat16).astype(F32)
        shares += [high, share - high]
    for m in range(8):
        rows = hyb_ref[m : m + 1, :]
        hit = jnp.broadcast_to(rows >> 7, (LANES, 512)) == sub
        lot = jnp.broadcast_to(rows & 127, (LANES, 512)) == sub
        left = jnp.concatenate([jnp.where(hit, jnp.broadcast_to(s, (LANES, 512)), 0.0).astype(jnp.bfloat16) for s in shares], 0)
        right = jnp.where(lot, 1.0, 0.0).astype(jnp.bfloat16)
        total = total + lax.dot_general(left, right, (((1,), (1,)), ((), ())), preferred_element_type=F32)
    for k in range(3):
        out[k] = total[2 * k * LANES : (2 * k + 1) * LANES] + total[(2 * k + 1) * LANES : (2 * k + 2) * LANES]


def comm_kernel(
    pos_hbm, zone_hbm, eps_hbm, mass_hbm, ghost_hbm, hyb_hbm,
    blocks_ref, prof_ref, spread_ref, local_ref, planes,
    zone_ref, mass_ref, ghost_ref, hyb_ref, bins, tables, sites,
    pay_ref, sums, part1, part2, got1, got2, mine, theirs, cols, pulls,
    load_sem, send_sem, recv_sem, s1, r1, s2, r2, ss, sr,
):
    group, slab_at, column = lax.axis_index("group"), lax.axis_index("gx"), lax.axis_index("yz")
    slab = group * 8 + slab_at

    loads = [
        pltpu.make_async_copy(src, dst, load_sem.at[i])
        for i, (src, dst) in enumerate((
            (pos_hbm, planes.at[0:3]), (zone_hbm, zone_ref), (eps_hbm, planes.at[5]),
            (ghost_hbm, ghost_ref), (mass_hbm, mass_ref), (hyb_hbm, hyb_ref),
        ))
    ]
    for load in loads:
        load.start()

    def in_column(d):
        return (group, slab_at, lax.rem(column + d, 8))

    def across(d):
        return (lax.rem(group + d // 8, 2), lax.rem(slab_at + d % 8, 8), column)

    barrier = pltpu.get_barrier_semaphore()
    for d in range(1, 8):
        pl.semaphore_signal(barrier, inc=1, device_id=in_column(d), device_id_type=MESH)
    for d in range(1, 16):
        pl.semaphore_signal(barrier, inc=1, device_id=across(d), device_id_type=MESH)

    step = 512 // PIECES
    routes = (
        (1, None, across(1)),
        (7, None, across(7)),
        (3, None, in_column(1)),
        (5, None, in_column(7)),
        (0, 1, in_column(1)),
        (2, 1, in_column(7)),
        (6, 7, in_column(1)),
        (8, 7, in_column(7)),
    )

    def copy(index, p):
        block, source, target = routes[index]
        rows = pl.ds(p * step, step)
        src = pay_ref.at[rows] if source is None else blocks_ref.at[source, rows]
        return pltpu.make_async_remote_copy(
            src_ref=src, dst_ref=blocks_ref.at[block, rows],
            send_sem=send_sem.at[index, p], recv_sem=recv_sem.at[index, p],
            device_id=target, device_id_type=MESH,
        )

    def share1(d):
        return pltpu.make_async_remote_copy(
            src_ref=part1, dst_ref=got1.at[d], send_sem=s1.at[d], recv_sem=r1.at[d],
            device_id=in_column(d), device_id_type=MESH)

    def share2(d):
        return pltpu.make_async_remote_copy(
            src_ref=part2, dst_ref=got2.at[d], send_sem=s2.at[d], recv_sem=r2.at[d],
            device_id=across(d), device_id_type=MESH)

    def forward(p):
        for first, lot in ((0, (4, 5)), (1, (6, 7))):
            copy(first, p).wait_recv()
            for i in lot:
                copy(i, p).start()

    for i in range(3):
        loads[i].wait()

    def resolve(v, _):
        at = pl.ds(pl.multiple_of(v * 8, 8), 8)
        zone = zone_ref[at, :]
        lam = jnp.where(zone == 0, 1.0, jnp.where(zone == 1, jax.nn.sigmoid(2.0 * planes[0, at, :]), 0.0))
        planes[3, at, :] = planes[5, at, :] * jnp.where(group == 0, lam, 1.0 - lam)
        planes[4, at, :] = lam
        bins[at, :] = NBS * jax.nn.sigmoid(planes[0, at, :])
        return 0

    lax.fori_loop(0, 16, resolve, 0, unroll=4)
    site_tables(planes, tables)
    sites[...] = jnp.zeros_like(sites)
    for i in range(3, 6):
        loads[i].wait()
    pl.semaphore_wait(barrier, 22)

    def ghosts(v, _):
        ids = [ghost_ref[pl.ds(pl.multiple_of(v * 16 + 8 * i, 8), 8), :] for i in range(2)]
        index = [v * 2, jnp.minimum(v * 2 + 1, 14)]
        other = [i + (i >= slab).astype(jnp.int32) for i in index]
        accs = [jnp.zeros((8, LANES), F32)] * NBS

        def beside(r):
            if r % 4 == 0:
                far_term(bins, mass_ref, accs, slab, other[r // 64], r // 4 % 16)
            if r % 64 == 63:
                keep_bins(sums, other[r // 64], accs)
                accs[:] = [jnp.zeros((8, LANES), F32)] * NBS

        member_sites(hyb_ref, tables, sites, v)
        out = lane_pick(planes, ids, beside)
        for i in range(2):
            dense_tiles(out[i], pay_ref, v * 2 + i)
            at = pl.ds(pl.multiple_of(v * 16 + 8 * i, 8), 8)
            dense_tiles([planes[k, at, :] for k in range(4)], local_ref, v * 2 + i)

        @pl.when(v % 2 == 1)
        def _():
            for i in range(4):
                copy(i, v // 2).start()

        @pl.when((v % 2 == 1) & (v >= 5))
        def _():
            forward(v // 2 - 2)

        return 0

    lax.fori_loop(0, 8, ghosts, 0)
    mine[...] = jnp.zeros_like(mine)
    for k in range(5):
        mine[k : k + 1, :] = jnp.sum(sites[k], axis=0, keepdims=True) * 0.125
    swap = pltpu.make_async_remote_copy(
        src_ref=mine, dst_ref=theirs, send_sem=ss, recv_sem=sr, device_id=across(8), device_id_type=MESH)
    swap.start()
    density(bins, mass_ref, slab, sums, part1)
    for d in range(1, 8):
        share1(d).start()
    forward(PIECES - 2)
    forward(PIECES - 1)
    swap.wait_recv()
    coupling(mine, theirs, cols, pulls)
    for d in range(1, 8):
        share1(d).wait_recv()
    total = part1[...]
    for d in range(1, 8):
        total = total + got1[d]
    part2[...] = total
    for d in range(1, 16):
        share2(d).start()
    spread(pulls, hyb_ref, spread_ref)
    for d in range(1, 16):
        share2(d).wait_recv()
    total = part2[...]
    for d in range(1, 16):
        total = total + got2[d]
    prof_ref[...] = total
    for p in range(PIECES):
        for i in range(2, 8):
            copy(i, p).wait_recv()
    for p in range(PIECES):
        for i in range(8):
            copy(i, p).wait_send()
    for d in range(1, 8):
        share1(d).wait_send()
    for d in range(1, 16):
        share2(d).wait_send()
    swap.wait_send()


def force_kernel(
    nb_hbm, local_ref, blocks_ref, prof_ref, spread_ref, planes,
    out_ref,
    nb_ref, table, turned, gathered, lots, forces, push, coef_a, coef_b, load_sem,
):
    group = lax.axis_index("group")
    slab = group * 8 + lax.axis_index("gx")
    load = pltpu.make_async_copy(nb_hbm, nb_ref, load_sem.at[0])
    load.start()
    lane = iota((8, LANES), 1)
    quarter = lane // 32

    def fill(source, block):
        def one(r, _):
            for u in range(16):
                rows = source[pl.ds(pl.multiple_of(r * 128 + u * 8, 8), 8), :]
                rolled = [rows] + [pltpu.roll(rows, 32 * k, 1) for k in (1, 2, 3)]
                at = block * 2048 + r * 512 + (u // 4) * 128 + u % 4
                for q in range(4):
                    tile = jnp.where(
                        quarter < 2,
                        jnp.where(quarter == 0, rolled[-q % 4], rolled[(1 - q) % 4]),
                        jnp.where(quarter == 2, rolled[(2 - q) % 4], rolled[(3 - q) % 4]),
                    )
                    table[pl.ds(at + q * 4, 8, stride=16), :] = tile
            return 0

        lax.fori_loop(0, 4, one, 0)

    fill(local_ref, 0)

    def ghost_fill(index, _):
        block = index + (index >= 4).astype(jnp.int32)
        fill(blocks_ref.at[block], block + 1)
        return 0

    lax.fori_loop(0, 8, ghost_fill, 0)
    table[20480:20488, :] = jnp.zeros((8, LANES), F32)
    for k in range(4):
        turned[k] = planes[k].T

    profile = prof_ref[...]
    mean = jnp.sum(profile) / 256.0
    for half in range(2):
        source, _, steps = order_of(slab, lane, half)
        steps = steps.astype(F32)
        dev = wide(profile[half : half + 1, :] / mean - 1.0)
        dev = jnp.take_along_axis(dev, source, axis=1) * weight_of(steps)
        coef_a[half * LANES : (half + 1) * LANES, :] = wide(dev[0:1, :], LANES).T
        coef_b[half * LANES : (half + 1) * LANES, :] = wide((dev * steps)[0:1, :], LANES).T

    def horner(q, start, count):
        a = wide(coef_a[pl.ds(start + count - 1, 1), :])
        b = wide(coef_b[pl.ds(start + count - 1, 1), :])
        for n in range(count - 2, -1, -1):
            a = a * q + wide(coef_a[pl.ds(start + n, 1), :])
            b = b * q + wide(coef_b[pl.ds(start + n, 1), :])
        return a, b

    def thermo_part(t, index):
        if index < 15:
            other = index + (index >= slab).astype(jnp.int32)
            dist = edge_distance(t, slab, other)
            a, b = horner(jnp.exp(-dist), other * NBS, NBS)
            part = jnp.exp(-0.5 * dist * (dist + 1.0)) * ((dist + 0.5) * a + b)
            return jnp.where(other > slab, -part, part)
        u = t - NEAR
        a, b = horner(jnp.exp(u), slab * NBS, NEAR)
        upper = jnp.exp(-0.5 * u * (u - 1.0)) * ((u - 0.5) * a - b)
        a, b = horner(jnp.exp(-u), slab * NBS + NEAR, NEAR)
        return upper + jnp.exp(-0.5 * u * (u + 1.0)) * ((u + 0.5) * a + b)

    def take(slot, cl):
        g = slot % 4
        for c in range(LANES):
            flat = (slot // 8) * 16384 + (c // 8) * 1024 + (slot % 8) * 128 + (c % 8) * 16
            tile = nb_ref.at[pl.ds(flat, 16)][cl]
            gathered[slot // 4, c : c + 1, 32 * g : 32 * g + 32] = table[pl.ds(tile, 1), 32 * g : 32 * g + 32]

    def pairs(curve, i, cl, slots, total):
        own = [wide(turned[k, pl.ds(cl * 8 + i, 1), :]) for k in range(3)]
        for slot in slots:
            quad, g = slot // 4, slot % 4
            at = [lots[quad, 32 * g + 8 * k : 32 * g + 8 * k + 8, :] for k in range(4)]
            d = [own[k] - at[k] for k in range(3)]
            w = at[3] * curve(d[0] * d[0] + d[1] * d[1] + d[2] * d[2])
            total = [total[k] + w * d[k] for k in range(3)]
        return total

    def keep(cl, accs):
        at = pl.ds(pl.multiple_of(cl * 8, 8), 8)
        charge = turned[3, at, :]
        for k in range(3):
            forces[k, at, :] = charge * fold8([acc[k] for acc in accs])

    def run(curve):
        zero = [jnp.zeros((8, LANES), F32)] * 3

        def body(cl, _):
            for quad in range(4):
                lots[quad] = gathered[quad].T
            before = jnp.maximum(cl - 1, 0)
            at = pl.ds(pl.multiple_of(cl * 8, 8), 8)
            t = NBS * jax.nn.sigmoid(planes[0, at, :])
            push_sum = jnp.zeros((8, LANES), F32)
            accs = [zero] * 8
            for slot in range(16):
                i, first = slot // 2, slot % 2 * 8
                accs[i] = pairs(curve, i, before, range(first, first + 8), accs[i])
                push_sum = push_sum + thermo_part(t, slot)
                take(slot, cl)
            lam = planes[4, at, :]
            push[at, :] = -4.0 * lam * (1.0 - lam) * push_sum
            keep(before, accs)
            return 0

        lax.fori_loop(0, 16, body, 0)
        for quad in range(4):
            lots[quad] = gathered[quad].T
        keep(15, [pairs(curve, i, 15, range(16), zero) for i in range(8)])

    def soft(s):
        r = 1.0 / (1.0 + s)
        return r * r * r

    gathered[...] = jnp.zeros_like(gathered)
    load.wait()

    @pl.when(group == 0)
    def _():
        run(soft)

    @pl.when(group != 0)
    def _():
        run(lambda s: jnp.exp(-0.5 * s))

    for k in range(3):
        plane = forces[k].T + spread_ref[k]
        if k == 0:
            plane = plane + push[...]
        out_ref[k] = plane


VMEM = pl.BlockSpec(memory_space=pltpu.VMEM)
ANY = pl.BlockSpec(memory_space=pl.ANY)
HBM = pl.BlockSpec(memory_space=pltpu.HBM)


def shape(*dims):
    return jax.ShapeDtypeStruct(dims, F32)


def per_device(site_pos, zone_id, site_eps, site_mass, neighbours, ghost_rows, hyb_map):
    pos = site_pos.reshape(3, 128, 128)
    zone = zone_id.reshape(128, 128)
    eps = site_eps.reshape(128, 128)
    mass = site_mass.reshape(128, 128)
    lists = neighbours.reshape(2, 8, 16, 128).transpose(0, 2, 1, 3).reshape(32768)
    ghost = ghost_rows.reshape(128, 128)
    hyb = hyb_map.reshape(8, 512)
    blocks, prof, extra, local, state = pl.pallas_call(
        comm_kernel,
        out_shape=(shape(9, 512, 128), shape(8, 128), shape(3, 128, 128), shape(512, 128), shape(6, 128, 128)),
        in_specs=[HBM] * 6,
        out_specs=(ANY, VMEM, VMEM, VMEM, VMEM),
        scratch_shapes=[
            pltpu.VMEM((128, 128), jnp.int32),
            pltpu.VMEM((128, 128), F32),
            pltpu.VMEM((128, 128), jnp.int32),
            pltpu.VMEM((8, 512), jnp.int32),
            pltpu.VMEM((128, 128), F32),
            pltpu.VMEM((3, 320, 256), jnp.bfloat16),
            pltpu.VMEM((5, 8, 512), F32),
            pltpu.VMEM((512, 128), F32),
            pltpu.VMEM((256, 128), F32),
            pltpu.VMEM((8, 128), F32),
            pltpu.VMEM((8, 128), F32),
            pltpu.VMEM((8, 8, 128), F32),
            pltpu.VMEM((16, 8, 128), F32),
            pltpu.VMEM((8, 512), F32),
            pltpu.VMEM((8, 512), F32),
            pltpu.VMEM((512, 128), F32),
            pltpu.VMEM((8, 512), F32),
            pltpu.SemaphoreType.DMA((6,)),
            pltpu.SemaphoreType.DMA((8, PIECES)),
            pltpu.SemaphoreType.DMA((8, PIECES)),
            pltpu.SemaphoreType.DMA((8,)),
            pltpu.SemaphoreType.DMA((8,)),
            pltpu.SemaphoreType.DMA((16,)),
            pltpu.SemaphoreType.DMA((16,)),
            pltpu.SemaphoreType.DMA,
            pltpu.SemaphoreType.DMA,
        ],
        compiler_params=pltpu.CompilerParams(
            collective_id=0, has_side_effects=True, vmem_limit_bytes=62 * 2**20
        ),
        name="exchange",
    )(pos, zone, eps, mass, ghost, hyb)
    forces = pl.pallas_call(
        force_kernel,
        out_shape=shape(3, 128, 128),
        in_specs=[HBM, VMEM, VMEM, VMEM, VMEM, VMEM],
        out_specs=VMEM,
        scratch_shapes=[
            pltpu.SMEM((32768,), jnp.int32),
            pltpu.VMEM((20488, 128), F32),
            pltpu.VMEM((4, 128, 128), F32),
            pltpu.VMEM((4, 128, 128), F32),
            pltpu.VMEM((4, 128, 128), F32),
            pltpu.VMEM((3, 128, 128), F32),
            pltpu.VMEM((128, 128), F32),
            pltpu.VMEM((256, 128), F32),
            pltpu.VMEM((256, 128), F32),
            pltpu.SemaphoreType.DMA((1,)),
        ],
        compiler_params=pltpu.CompilerParams(vmem_limit_bytes=56 * 2**20),
        name="forces",
    )(lists, local, blocks, prof, extra, state)
    return forces.reshape(1, 1, 1, 3, 16384)


def solution(mesh):
    return jax.shard_map(
        per_device,
        mesh=mesh,
        in_specs=(
            P("group", "gx", "yz", None, None),
            P("group", "gx", "yz", None),
            P("group", "gx", "yz", None),
            P("group", "gx", "yz", None),
            P("group", "gx", "yz", None, None),
            P("group", "gx", "yz", None),
            P("group", "gx", "yz", None, None),
        ),
        out_specs=P("group", "gx", "yz", None, None),
        check_vma=False,
    )
```

time: 96.3 us -> 67.3 us (0.70)
  Pallas kernels: 87.1 us -> 66.8 us
  local copies, waits for them, and re-layouts: 8.61 us -> 0 us
    pallas_call x2 -> x1, Pallas kernels: 55.9 us -> 31.7 us  [per_device(): pl.pallas_call(force_kernel, out_shape=shape(3, 128, 128), in_specs=[HBM,...]
    unnamed x16 -> x0, local copies, waits for them, and re-layouts: 7.73 us -> none
    pallas_call x1, Pallas kernels: 31.2 us -> 35.2 us  [per_device(): pl.pallas_call(comm_kernel, out_shape=(shape(9, 512, 128), shape(8, 128),...]
where the time goes in v2:
time: 67.3 us; the launch traced here: 66.8 us
  Pallas kernels  66.8 us (99%)
    pallas_call x1, Pallas kernels, per_device(): pl.pallas_call(comm_kernel, out_shape=(shape(9, 512, 128), shape(8, 128),...  35.2 us
    pallas_call x1, Pallas kernels, per_device(): pl.pallas_call(force_kernel, out_shape=shape(3, 128, 128), in_specs=[HBM,...  31.7 us

profile of v2, /device:TPU:1, one launch (start us, length us, event | category | flops | bytes accessed | tf_op | source)
XLA Modules:
  0.0 66.8 jit_solution(15083241047425884968)
XLA Ops:
  0.0 35.2 %exchange.1 = (f32[9,512,128]{2,1,0:T(8,128)}, f32[8,128]{1,0:T(8,128)}, f32[3,128,128]{2,1,0:T(8,128)}, f32[512,128]{1,0:T(8,128)}, f32[6,128,128]{2,1,0:T(8,128)}) custom-call(f32[3,128,128]{2,1,0:T(8,128)} %bitcast.12, s32[128,128]{1,0:T(8,128)} %bitcast.14, f32[128,128]{1,0:T(8,128)} %bitcast.15, f32[128,128]{1,0:T(8,128)} %bitcast.16, ...), custom_call_target="tpu_custom_call" | custom-call | tf_op jit(solution)/shard_map/exchange/pallas_call | solution.py:514
  35.2 31.7 %forces.1 = f32[3,128,128]{2,1,0:T(8,128)} custom-call(s32[32768]{0:T(1024)} %bitcast.13, f32[512,128]{1,0:T(8,128)} %get-tuple-element.10.local_ref, f32[9,512,128]{2,1,0:T(8,128)} %get-tuple-element.11.blocks_ref, f32[8,128]{1,0:T(8,128)} %get-tuple-element.12.prof_ref, f32[3,128,128]{2,1,0:T(8,128)} %get-tuple-element.13.spread_ref, ...), custom_call_target="tpu_custom_call" | custom-call | tf_op jit(solution)/shard_map/forces/pallas_call | solution.py:552

commit v3 on v2

--- a/solution.py
+++ b/solution.py
@@ -164,7 +164,7 @@
                 accs[w * 3 + k] = accs[w * 3 + k] + weight * d[k]
         return tuple(accs)
 
-    accs = lax.fori_loop(0, 64, step, (jnp.zeros((8, LANES), F32),) * 12)
+    accs = lax.fori_loop(0, 64, step, (jnp.zeros((8, LANES), F32),) * 12, unroll=8)
     for w in range(4):
         for k in range(3):
             pulls[k : k + 1, w * LANES : (w + 1) * LANES] = jnp.sum(accs[w * 3 + k], axis=0, keepdims=True) * (0.5 * 4.0 / 512)
@@ -177,12 +177,14 @@
     for k in range(3):
         share = pulls[k : k + 1, :] * 0.125
         high = share.astype(jnp.bfloat16).astype(F32)
-        shares += [high, share - high]
+        for part in (high, share - high):
+            shares.append(jnp.broadcast_to(part, (LANES, 512)).astype(jnp.bfloat16))
     for m in range(8):
         rows = hyb_ref[m : m + 1, :]
         hit = jnp.broadcast_to(rows >> 7, (LANES, 512)) == sub
         lot = jnp.broadcast_to(rows & 127, (LANES, 512)) == sub
-        left = jnp.concatenate([jnp.where(hit, jnp.broadcast_to(s, (LANES, 512)), 0.0).astype(jnp.bfloat16) for s in shares], 0)
+        hot = jnp.where(hit, 1.0, 0.0).astype(jnp.bfloat16)
+        left = jnp.concatenate([hot * s for s in shares], 0)
         right = jnp.where(lot, 1.0, 0.0).astype(jnp.bfloat16)
         total = total + lax.dot_general(left, right, (((1,), (1,)), ((), ())), preferred_element_type=F32)
     for k in range(3):
@@ -190,8 +192,8 @@
 
 
 def comm_kernel(
-    pos_hbm, zone_hbm, eps_hbm, mass_hbm, ghost_hbm, hyb_hbm,
-    blocks_ref, prof_ref, spread_ref, local_ref, planes,
+    pos_hbm, zone_hbm, eps_hbm, mass_hbm, ghost_hbm, hyb_hbm, list_hbm,
+    blocks_ref, prof_ref, spread_ref, local_ref, planes, rows_ref,
     zone_ref, mass_ref, ghost_ref, hyb_ref, bins, tables, sites,
     pay_ref, sums, part1, part2, got1, got2, mine, theirs, cols, pulls,
     load_sem, send_sem, recv_sem, s1, r1, s2, r2, ss, sr,
@@ -203,7 +205,7 @@
         pltpu.make_async_copy(src, dst, load_sem.at[i])
         for i, (src, dst) in enumerate((
             (pos_hbm, planes.at[0:3]), (zone_hbm, zone_ref), (eps_hbm, planes.at[5]),
-            (ghost_hbm, ghost_ref), (mass_hbm, mass_ref), (hyb_hbm, hyb_ref),
+            (ghost_hbm, ghost_ref), (mass_hbm, mass_ref), (hyb_hbm, hyb_ref), (list_hbm, rows_ref),
         ))
     ]
     for load in loads:
@@ -310,6 +312,9 @@
         return 0
 
     lax.fori_loop(0, 8, ghosts, 0)
+    loads[6].wait()
+    tile = rows_ref[...]
+    rows_ref[...] = (tile & -128) | ((tile & 3) << 5) | (((tile >> 2) & 3) << 3) | ((tile >> 4) & 7)
     mine[...] = jnp.zeros_like(mine)
     for k in range(5):
         mine[k : k + 1, :] = jnp.sum(sites[k], axis=0, keepdims=True) * 0.125
@@ -320,9 +325,9 @@
     for d in range(1, 8):
         share1(d).start()
     forward(PIECES - 2)
-    forward(PIECES - 1)
     swap.wait_recv()
     coupling(mine, theirs, cols, pulls)
+    forward(PIECES - 1)
     for d in range(1, 8):
         share1(d).wait_recv()
     total = part1[...]
@@ -368,14 +373,14 @@
             for u in range(16):
                 rows = source[pl.ds(pl.multiple_of(r * 128 + u * 8, 8), 8), :]
                 rolled = [rows] + [pltpu.roll(rows, 32 * k, 1) for k in (1, 2, 3)]
-                at = block * 2048 + r * 512 + (u // 4) * 128 + u % 4
+                at = pl.multiple_of(block * 2048 + r * 512 + u * 32, 8)
                 for q in range(4):
                     tile = jnp.where(
                         quarter < 2,
                         jnp.where(quarter == 0, rolled[-q % 4], rolled[(1 - q) % 4]),
                         jnp.where(quarter == 2, rolled[(2 - q) % 4], rolled[(3 - q) % 4]),
                     )
-                    table[pl.ds(at + q * 4, 8, stride=16), :] = tile
+                    table[pl.ds(at + q * 8, 8), :] = tile
             return 0
 
         lax.fori_loop(0, 4, one, 0)
@@ -473,7 +478,9 @@
         keep(15, [pairs(curve, i, 15, range(16), zero) for i in range(8)])
 
     def soft(s):
-        r = 1.0 / (1.0 + s)
+        near = 1.0 + s
+        r = pl.reciprocal(near, approx=True)
+        r = r * (2.0 - near * r)
         return r * r * r
 
     gathered[...] = jnp.zeros_like(gathered)
@@ -508,14 +515,14 @@
     zone = zone_id.reshape(128, 128)
     eps = site_eps.reshape(128, 128)
     mass = site_mass.reshape(128, 128)
-    lists = neighbours.reshape(2, 8, 16, 128).transpose(0, 2, 1, 3).reshape(32768)
+    lists = neighbours.reshape(2, 8, 16, 128).transpose(0, 2, 1, 3).reshape(256, 128)
     ghost = ghost_rows.reshape(128, 128)
     hyb = hyb_map.reshape(8, 512)
-    blocks, prof, extra, local, state = pl.pallas_call(
+    blocks, prof, extra, local, state, rows = pl.pallas_call(
         comm_kernel,
-        out_shape=(shape(9, 512, 128), shape(8, 128), shape(3, 128, 128), shape(512, 128), shape(6, 128, 128)),
-        in_specs=[HBM] * 6,
-        out_specs=(ANY, VMEM, VMEM, VMEM, VMEM),
+        out_shape=(shape(9, 512, 128), shape(8, 128), shape(3, 128, 128), shape(512, 128), shape(6, 128, 128), jax.ShapeDtypeStruct((256, 128), jnp.int32)),
+        in_specs=[HBM] * 7,
+        out_specs=(ANY, VMEM, VMEM, VMEM, VMEM, VMEM),
         scratch_shapes=[
             pltpu.VMEM((128, 128), jnp.int32),
             pltpu.VMEM((128, 128), F32),
@@ -534,7 +541,7 @@
             pltpu.VMEM((8, 512), F32),
             pltpu.VMEM((512, 128), F32),
             pltpu.VMEM((8, 512), F32),
-            pltpu.SemaphoreType.DMA((6,)),
+            pltpu.SemaphoreType.DMA((7,)),
             pltpu.SemaphoreType.DMA((8, PIECES)),
             pltpu.SemaphoreType.DMA((8, PIECES)),
             pltpu.SemaphoreType.DMA((8,)),
@@ -548,7 +555,7 @@
             collective_id=0, has_side_effects=True, vmem_limit_bytes=62 * 2**20
         ),
         name="exchange",
-    )(pos, zone, eps, mass, ghost, hyb)
+    )(pos, zone, eps, mass, ghost, hyb, lists)
     forces = pl.pallas_call(
         force_kernel,
         out_shape=shape(3, 128, 128),
@@ -568,7 +575,7 @@
         ],
         compiler_params=pltpu.CompilerParams(vmem_limit_bytes=56 * 2**20),
         name="forces",
-    )(lists, local, blocks, prof, extra, state)
+    )(rows.reshape(32768), local, blocks, prof, extra, state)
     return forces.reshape(1, 1, 1, 3, 16384)
 
 

time: 67.3 us -> 62.7 us (0.932)
  Pallas kernels: 66.8 us -> 62.6 us
    pallas_call x1, Pallas kernels: 35.2 us -> 31.1 us  [per_device(): pl.pallas_call(comm_kernel, out_shape=(shape(9, 512, 128), shape(8, 128),...]
where the time goes in v3:
time: 62.7 us; the launch traced here: 62.6 us
  Pallas kernels  62.6 us (100%)
    pallas_call x1, Pallas kernels, per_device(): pl.pallas_call(force_kernel, out_shape=shape(3, 128, 128), in_specs=[HBM,...  31.5 us
    pallas_call x1, Pallas kernels, per_device(): pl.pallas_call(comm_kernel, out_shape=(shape(9, 512, 128), shape(8, 128),...  31.1 us

profile of v3, /device:TPU:1, one launch (start us, length us, event | category | flops | bytes accessed | tf_op | source)
XLA Modules:
  0.0 62.6 jit_solution(14688156666736270036)
XLA Ops:
  0.0 31.1 %exchange.1 = (f32[9,512,128]{2,1,0:T(8,128)}, f32[8,128]{1,0:T(8,128)}, f32[3,128,128]{2,1,0:T(8,128)}, f32[512,128]{1,0:T(8,128)}, f32[6,128,128]{2,1,0:T(8,128)}, /*index=5*/s32[256,128]{1,0:T(8,128)}) custom-call(f32[3,128,128]{2,1,0:T(8,128)} %bitcast.13, s32[128,128]{1,0:T(8,128)} %bitcast.16, f32[128,128]{1,0:T(8,128)} %bitcast.17, ...), custom_call_target="tpu_custom_call" | custom-call | tf_op jit(solution)/shard_map/exchange/pallas_call | solution.py:521
  31.1 31.5 %forces.1 = f32[3,128,128]{2,1,0:T(8,128)} custom-call(s32[32768]{0:T(1024)} %bitcast.15, f32[512,128]{1,0:T(8,128)} %get-tuple-element.12.local_ref, f32[9,512,128]{2,1,0:T(8,128)} %get-tuple-element.13.blocks_ref, f32[8,128]{1,0:T(8,128)} %get-tuple-element.14.prof_ref, f32[3,128,128]{2,1,0:T(8,128)} %get-tuple-element.15.spread_ref, ...), custom_call_target="tpu_custom_call" | custom-call | tf_op jit(solution)/shard_map/forces/pallas_call | solution.py:559

commit v4 on v3

--- a/solution.py
+++ b/solution.py
@@ -293,8 +293,8 @@
                 keep_bins(sums, other[r // 64], accs)
                 accs[:] = [jnp.zeros((8, LANES), F32)] * NBS
 
+        out = lane_pick(planes, ids, beside)
         member_sites(hyb_ref, tables, sites, v)
-        out = lane_pick(planes, ids, beside)
         for i in range(2):
             dense_tiles(out[i], pay_ref, v * 2 + i)
             at = pl.ds(pl.multiple_of(v * 16 + 8 * i, 8), 8)

time: 62.7 us -> 62.7 us (level)
  no operation moved by 1% of the time
where the time goes in v4:
time: 62.7 us; the launch traced here: 62.6 us
  Pallas kernels  62.5 us (100%)
    pallas_call x1, Pallas kernels, per_device(): pl.pallas_call(force_kernel, out_shape=shape(3, 128, 128), in_specs=[HBM,...  31.5 us
    pallas_call x1, Pallas kernels, per_device(): pl.pallas_call(comm_kernel, out_shape=(shape(9, 512, 128), shape(8, 128),...  31.1 us

profile of v4, /device:TPU:1, one launch (start us, length us, event | category | flops | bytes accessed | tf_op | source)
XLA Modules:
  0.0 62.6 jit_solution(5097216506409594382)
XLA Ops:
  0.0 31.1 %exchange.1 = (f32[9,512,128]{2,1,0:T(8,128)}, f32[8,128]{1,0:T(8,128)}, f32[3,128,128]{2,1,0:T(8,128)}, f32[512,128]{1,0:T(8,128)}, f32[6,128,128]{2,1,0:T(8,128)}, /*index=5*/s32[256,128]{1,0:T(8,128)}) custom-call(f32[3,128,128]{2,1,0:T(8,128)} %bitcast.13, s32[128,128]{1,0:T(8,128)} %bitcast.16, f32[128,128]{1,0:T(8,128)} %bitcast.17, ...), custom_call_target="tpu_custom_call" | custom-call | tf_op jit(solution)/shard_map/exchange/pallas_call | solution.py:521
  31.1 31.5 %forces.1 = f32[3,128,128]{2,1,0:T(8,128)} custom-call(s32[32768]{0:T(1024)} %bitcast.15, f32[512,128]{1,0:T(8,128)} %get-tuple-element.12.local_ref, f32[9,512,128]{2,1,0:T(8,128)} %get-tuple-element.13.blocks_ref, f32[8,128]{1,0:T(8,128)} %get-tuple-element.14.prof_ref, f32[3,128,128]{2,1,0:T(8,128)} %get-tuple-element.15.spread_ref, ...), custom_call_target="tpu_custom_call" | custom-call | tf_op jit(solution)/shard_map/forces/pallas_call | solution.py:559
